TPU v7x, 32 devices: a whole 2x2x4 slice. The times are simulated.
32 devices in a mesh: group: 2 (over y), seq: 4 (over z), shard: 2 (over x), guide: 2 (over core).
Axes of the slice: x: 2, y: 2, z: 4, core: 2. Of those that a mesh axis runs over, the one named last changes fastest.
Arguments:
- queries: bfloat16 [2, 2, 512, 2560], P('guide', 'group', 'seq', 'shard'), parts along dimension 1, may hold values from -120 to 120
- key_vecs: bfloat16 [2, 2, 512, 2560], P('guide', 'group', 'seq', 'shard'), parts along dimension 1, may hold values from -4 to 4
- value_vecs: bfloat16 [2, 2, 512, 2560], P('guide', 'group', 'seq', 'shard'), parts along dimension 1, may hold values from -24 to 24
- residual: bfloat16 [2, 2, 512, 5120], P('guide', 'group', 'seq', 'shard'), parts along dimension 1, may hold values from -64 to 64
- w_out: bfloat16 [2560, 5120], P('shard', 'guide'), may hold values from -0.125 to 0.125
- attn_gate: float32 [2, 5120], P('group', 'shard'), parts along dimension 0, may hold values from 2 to 4
- norm_shift: float32 [2, 5120], P('group', 'shard'), parts along dimension 0, may hold values from -3 to 3
- norm_scale: float32 [2, 5120], P('group', 'shard'), parts along dimension 0, may hold values from -2.5 to 2.5
- w_head: bfloat16 [5120, 64], P('shard'), may hold values from -0.078125 to 0.078125
- noise: float32 [2, 4, 128, 64], P('group', 'seq', None, 'guide'), parts along dimension 0, may hold values from -6 to 6
- timesteps: int32 [2], P('group'), parts along dimension 0, may hold values from 100 to 980
- frame_owner: int32 [2, 4], P('group'), parts along dimension 0, may hold values from 0 to 3, each once within a row
Outputs:
- sds_grad: float32 [2, 4, 128, 64], P('group', 'seq', None, 'guide'), parts along dimension 0
There are 2 independent parts, one for each index of `group`. A program takes and returns all parts, laid end to end along the dimension named above; an argument that names none is the same for every part. Nothing has to cross between parts.
Inputs may be any that keep to these rules, and one draw needn't show every extreme that they name: `frame_owner`: each row names every owner index once.
All inputs are finite; a program needn't handle non-finite values.
Results may differ from a plain program's by a relative error of at most 0.003.
Values may be sent and summed in bfloat16 or wider, within the bound.
A program may use at most 128 MiB of HBM per device.

v0:
```python
import jax
import jax.numpy as jnp
from jax import lax
from jax.sharding import PartitionSpec as P

D = 5120
HEAD_DIM = 128


beta_low = 0.0001
beta_high = 0.02
guidance_scale = 3.0
norm_epsilon = 1e-06


def plan_weight(timesteps):
    steps_float = timesteps.astype(jnp.float32)
    exponent = (steps_float + 1.0) * beta_low + (beta_high - beta_low) * steps_float * (
        steps_float + 1.0
    ) / (2.0 * 999.0)
    return 1.0 - jnp.exp(-exponent)


def softmax_absorb(query_block, carry_state, pieces):
    running_top, running_total, running_acc = carry_state
    keys_block, values_block = pieces
    heads_local = query_block.shape[2]
    keys_split = keys_block.reshape(keys_block.shape[0], keys_block.shape[1], heads_local, HEAD_DIM)
    values_split = values_block.reshape(
        values_block.shape[0], values_block.shape[1], heads_local, HEAD_DIM
    )
    scores = jnp.einsum(
        "tqhd,tkhd->tqhk", query_block, keys_split, preferred_element_type=jnp.float32
    ) * HEAD_DIM ** (-0.5)
    new_top = jnp.max(scores, axis=-1)
    factor = jnp.exp(running_top - new_top)
    expo = jnp.exp(scores - new_top[..., None])
    new_total = running_total * factor + jnp.sum(expo, axis=-1)
    update = jnp.einsum(
        "tqhk,tkhd->tqhd",
        expo.astype(jnp.bfloat16),
        values_split,
        preferred_element_type=jnp.float32,
    )
    return (new_top, new_total, running_acc * factor[..., None] + update)


def start_state(step_count, token_count, heads_local):
    return (
        jnp.full((step_count, token_count, heads_local), -jnp.inf, jnp.float32),
        jnp.zeros((step_count, token_count, heads_local), jnp.float32),
        jnp.zeros((step_count, token_count, heads_local, HEAD_DIM), jnp.float32),
    )


def on_device(
    queries,
    key_vecs,
    value_vecs,
    residual,
    w_out,
    attn_gate,
    norm_shift,
    norm_scale,
    w_head,
    noise,
    timesteps,
    frame_owner,
):
    query_local = queries[0]
    step_count, token_count, width_local = query_local.shape
    heads_local = width_local // HEAD_DIM
    query_split = query_local.reshape(step_count, token_count, heads_local, HEAD_DIM)
    final_state = softmax_absorb(
        query_split,
        start_state(step_count, token_count, heads_local),
        (
            lax.all_gather(key_vecs[0], "seq", axis=1, tiled=True),
            lax.all_gather(value_vecs[0], "seq", axis=1, tiled=True),
        ),
    )
    total_sum = final_state[1]
    acc_sum = final_state[2]
    row_count = step_count * token_count
    attended = (acc_sum / total_sum[..., None]).astype(jnp.bfloat16).reshape(row_count, width_local)
    both_rows = jnp.dot(
        lax.all_gather(attended, "guide", axis=0, tiled=True),
        w_out,
        preferred_element_type=jnp.float32,
    )
    half_width = w_out.shape[1]
    swapped = lax.all_to_all(
        both_rows.reshape(2, row_count, half_width),
        "guide",
        split_axis=0,
        concat_axis=2,
        tiled=True,
    )
    projected = swapped.reshape(row_count, 2 * half_width)
    attn_out = lax.psum_scatter(projected, "shard", scatter_dimension=1, tiled=True)
    width_shard = attn_out.shape[1]
    hidden = residual[0].astype(jnp.float32) + attn_gate[:, None, :] * attn_out.reshape(
        step_count, token_count, width_shard
    )
    sum_first = jnp.sum(hidden, axis=-1)
    sum_second = jnp.sum(hidden * hidden, axis=-1)
    sum_first, sum_second = lax.psum((sum_first, sum_second), "shard")
    mean_row = sum_first / D
    var_row = sum_second / D - mean_row * mean_row
    inv_std = lax.rsqrt(var_row + norm_epsilon)
    modulated = (hidden - mean_row[..., None]) * inv_std[..., None] * (
        1.0 + norm_scale[:, None, :]
    ) + norm_shift[:, None, :]
    head_float = w_head.astype(jnp.float32)
    partial_head = jnp.einsum("tqd,dc->tqc", modulated, head_float, precision=lax.Precision.HIGHEST)
    predicted = lax.psum(partial_head, "shard")
    seq_count = lax.axis_size("seq")
    frame_group = token_count // seq_count
    channels = predicted.shape[-1]
    frames_view = predicted.reshape(step_count, seq_count, frame_group, channels)
    owner_table = (
        frame_owner[:, :, None] == jnp.arange(seq_count, dtype=jnp.int32)[None, None, :]
    ).astype(jnp.float32)
    by_owner = jnp.einsum(
        "tfo,tfgc->togc", owner_table, frames_view, precision=lax.Precision.HIGHEST
    )
    weight = plan_weight(timesteps)
    arrived = lax.all_to_all(
        lax.all_to_all(by_owner[None], "seq", split_axis=2, concat_axis=3, tiled=True),
        "guide",
        split_axis=4,
        concat_axis=0,
        tiled=True,
    )
    guided = arrived[1] + guidance_scale * (arrived[0] - arrived[1])
    return weight[:, None, None, None] * (guided - noise)


def solution(mesh):
    return jax.shard_map(
        on_device,
        mesh=mesh,
        in_specs=(
            P("guide", "group", "seq", "shard"),
            P("guide", "group", "seq", "shard"),
            P("guide", "group", "seq", "shard"),
            P("guide", "group", "seq", "shard"),
            P("shard", "guide"),
            P("group", "shard"),
            P("group", "shard"),
            P("group", "shard"),
            P("shard", None),
            P("group", "seq", None, "guide"),
            P("group"),
            P("group", None),
        ),
        out_specs=P("group", "seq", None, "guide"),
        check_vma=False,
    )
```

profile of v0, /device:TPU:0, one launch (start us, length us, event | category | flops | bytes accessed | tf_op | source)
XLA Modules:
  0.0 175.6 jit_solution(11851235863250960437)
XLA Ops:
  6.5 0.0 copy-start
  6.5 0.0 copy-start.3
  6.5 0.0 all-gather.5.cloned.1.call-start
  6.5 1.9 %copy.44 = bf16[1,1,128,1280]{2,3,1,0:T(8,128)(2,1)} copy(bf16[1,1,128,1280]{3,2,1,0:T(8,128)(2,1)} %param.13) | data formatting | bytes 655360 | tf_op args[1]
  8.5 0.0 all-gather.5.cloned.1.call-update
  8.5 0.0 all-gather.7.cloned.1.call-start
  8.5 0.7 all-gather.7.cloned.1.call-update
  9.2 0.0 reduce-scatter.2.cloned.1.call-start
  9.3 0.0 copy-done.3
  9.3 0.2 copy.45
  9.5 35.6 %all-gather.5.cloned.1.call-done = bf16[1,1,512,1280]{2,3,1,0:T(8,128)(2,1)} async-done(((bf16[1,1,128,1280]{2,3,1,0:T(8,128)(2,1)}), bf16[1,1,512,1280]{2,3,1,0:T(8,128)(2,1)}) %all-gather.5.cloned.1.call-update) | async-done | bytes 1310736 | tf_op jit(solution)/shard_map/all_gather | solution.py:78
  45.1 1.9 %bitcast_reduce_fusion = (f32[128,10]{0,1:T(8,128)S(1)}, f32[10,512,128]{2,1,0:T(8,128)S(1)}) fusion(bf16[512,10,128]{0,2,1:T(8,128)(2,1)} %bitcast.120, bf16[128,10,128]{0,2,1:T(8,128)(2,1)S(1)} %bitcast.119), kind=kOutput, calls=%fused_computation.1 | convolution fusion | flops 169081600 | bytes 4264960 | tf_op jit(solution)/shard_map/tqhd,tkhd->tqhk/dot_general | solution.py:32
  47.0 0.4 fusion.1
  47.5 30.4 %all-gather.7.cloned.1.call-done = bf16[1,1,512,1280]{3,2,1,0:T(8,128)(2,1)} async-done(((bf16[1,1,128,1280]{3,2,1,0:T(8,128)(2,1)}), bf16[1,1,512,1280]{3,2,1,0:T(8,128)(2,1)}) %all-gather.7.cloned.1.call-update) | async-done | bytes 1310736 | tf_op jit(solution)/shard_map/all_gather | solution.py:79
  77.9 2.4 %copy.48 = bf16[1,1,512,1280]{2,3,1,0:T(8,128)(2,1)} copy(bf16[1,1,512,1280]{3,2,1,0:T(8,128)(2,1)} %all-gather.7.cloned.1.call-done) | data formatting | bytes 2621440 | tf_op jit(solution)/shard_map/all_gather | solution.py:79
  80.4 2.1 %fusion.22 = bf16[1,128,10,128]{1,3,2,0:T(8,128)(2,1)S(1)} fusion(bf16[512,10,128]{0,2,1:T(8,128)(2,1)} %bitcast.121, f32[10,512,128]{2,1,0:T(8,128)S(1)} %get-tuple-element.14, f32[128,10]{0,1:T(8,128)S(1)} %get-tuple-element.13, f32[128,10]{0,1:T(8,128)S(1)} %get-tuple-element.10, f32[128,10]{0,1:T(8,128)S(1)} %get-tuple-element.9), kind=kOutput, calls=%fused_computation.19 | convolution fusion | flops 170229760 | bytes 4275200 | tf_op jit(solution)/shard_map/tqhk,tkhd->tqhd/dot_general | solution.py:39
  82.4 2.3 %all_gather.11 = bf16[256,1280]{0,1:T(8,128)(2,1)S(1)} all-gather(bf16[128,1280]{0,1:T(8,128)(2,1)S(1)} %bitcast.122), channel_id=1, replica_groups=mesh['group'=2,'seq'=4,'shard'=2,'guide'=2] {'guide'}, dimensions={0}, use_global_device_ids=true | all-gather | bytes 983040 | tf_op jit(solution)/shard_map/all_gather | solution.py:87
  84.7 4.7 %fusion.40 = f32[256,2560]{1,0:T(8,128)S(1)} fusion(bf16[256,1280]{0,1:T(8,128)(2,1)S(1)} %all_gather.11, bf16[1280,2560]{1,0:T(8,128)(2,1)} %param.16), kind=kOutput, calls=%fused_computation.43 | convolution fusion | flops 1677721600 | bytes 9830400 | tf_op jit(solution)/shard_map/dot_general | solution.py:86
  89.4 5.8 %all_to_all.42 = f32[2,128,2560]{2,1,0:T(8,128)S(1)} all-to-all(f32[2,128,2560]{2,1,0:T(8,128)S(1)} %bitcast.115), channel_id=1, replica_groups=mesh['group'=2,'seq'=4,'shard'=2,'guide'=2] {'guide'}, dimensions={0} | all-to-all | bytes 5242880 | tf_op jit(solution)/shard_map/all_to_all | solution.py:92
  95.3 2.0 %copy.50 = f32[1,128,2,2560]{3,2,1,0:T(2,128)S(1)} copy(f32[1,128,2,2560]{3,1,2,0:T(8,128)S(1)} %bitcast.117) | data formatting | bytes 5242880 | tf_op jit(solution)/shard_map/all_to_all | solution.py:92
  97.3 2.0 %copy.63 = f32[16,8,2,2560]{3,1,2,0:T(8,128)} copy(f32[16,8,2,2560]{3,2,1,0:T(2,128)S(1)} %bitcast.118) | data formatting | bytes 5242880
  99.3 0.0 copy-start.5
  99.3 0.0 reduce-scatter.2.cloned.1.call-update
  99.3 0.7 copy-done.5
  100.0 0.0 copy-done.6
  100.1 0.0 copy-done.7
  100.1 35.9 %reduce-scatter.2.cloned.1.call-done = f32[128,2560]{1,0:T(8,128)} async-done(((f32[128,5120]{1,0:T(8,128)}), f32[128,2560]{1,0:T(8,128)}) %reduce-scatter.2.cloned.1.call-update) | async-done | bytes 1310736 | tf_op jit(solution)/shard_map/reduce_scatter | solution.py:100
  136.0 0.0 copy-done.2
  136.0 1.8 %fusion.29 = (f32[128]{0:T(128)S(1)}, f32[128]{0:T(128)S(1)}) fusion(f32[128,2560]{1,0:T(8,128)} %reduce-scatter.2.cloned.1.call-done, f32[2560]{0:T(1024)S(1)} %reduce.6, bf16[1,1,128,2560]{3,2,1,0:T(8,128)(2,1)S(1)} %copy-done.2), kind=kLoop, calls=%fused_computation.25 | loop fusion | flops 1965824 | bytes 1977344 | tf_op jit(solution)/shard_map/reduce_sum | solution.py:105
  137.8 4.9 %all-reduce = (f32[1,128]{1,0:T(1,128)S(1)}, f32[1,128]{1,0:T(1,128)S(1)}) all-reduce(f32[1,128]{1,0:T(1,128)S(1)} %bitcast.130, f32[1,128]{1,0:T(1,128)S(1)} %bitcast.129), channel_id=1, replica_groups=mesh['group'=2,'seq'=4,'shard'=2,'guide'=2] {'shard'}, use_global_device_ids=true, to_apply=%region_6.0 | all-reduce | flops 256 | bytes 2048 | tf_op jit(solution)/shard_map/psum | solution.py:107
  142.8 0.0 copy-done
  142.8 0.0 copy-done.1
  142.8 0.0 copy-start.8
  142.8 0.0 copy-start.4
  142.8 1.0 fusion.6
  143.9 7.7 %psum.23 = f32[4,32,64]{2,0,1:T(4,128)S(1)} all-reduce(f32[4,32,64]{2,0,1:T(4,128)S(1)} %copy.52), channel_id=1, replica_groups=mesh['group'=2,'seq'=4,'shard'=2,'guide'=2] {'shard'}, use_global_device_ids=true, to_apply=%region_7.0 | all-reduce | flops 8192 | bytes 65536 | tf_op jit(solution)/shard_map/psum | solution.py:116
  151.5 0.0 copy-done.8
  151.6 0.3 convolution_bitcast_fusion
  151.9 0.7 reshape.232
  152.6 5.0 %all-to-all-start.1 = ((f32[4,1,2048]{2,1,0:T(1,128)}), f32[4,1,2048]{2,1,0:T(1,128)S(1)}, u32[]{:S(2)}, u32[]{:S(2)}) async-start(f32[4,1,2048]{2,1,0:T(1,128)} %reshape.232), calls=%async_computation.2 | async-start | bytes 65536 | tf_op jit(solution)/shard_map/all_to_all | solution.py:129
  158.3 5.0 %all-to-all-done.1 = f32[4,1,2048]{2,1,0:T(1,128)S(1)} async-done(((f32[4,1,2048]{2,1,0:T(1,128)}), f32[4,1,2048]{2,1,0:T(1,128)S(1)}, u32[]{:S(2)}, u32[]{:S(2)}) %all-to-all-start.1) | async-done | bytes 32800 | tf_op jit(solution)/shard_map/all_to_all | solution.py:129
  163.2 0.5 broadcast.99
  163.8 0.7 reduce.10
  164.5 0.1 reshape.233
  164.6 0.1 copy.55
  164.6 3.8 %all_to_all.43 = f32[1,1,1,128,64]{3,2,1,0,4:T(1,128)S(1)} all-to-all(f32[1,1,1,128,64]{3,2,1,0,4:T(1,128)S(1)} %copy.55), channel_id=1, replica_groups=mesh['group'=2,'seq'=4,'shard'=2,'guide'=2] {'guide'}, dimensions={4} | all-to-all | bytes 65536 | tf_op jit(solution)/shard_map/all_to_all | solution.py:128
  168.4 0.0 copy-done.4
  168.4 0.6 fusion.34
  (11 shorter events, 0.2 us)
Async XLA Ops:
  6.5 136.2 %copy-start = (bf16[2560,64]{0,1:T(8,128)(2,1)S(1)}, bf16[2560,64]{0,1:T(8,128)(2,1)}, u32[]{:S(2)}) copy-start(bf16[2560,64]{0,1:T(8,128)(2,1)} %param.20) | copy-start | bytes 983044
  6.5 2.8 %copy-start.3 = (bf16[1,1,128,1280]{3,2,1,0:T(8,128)(2,1)S(1)}, bf16[1,1,128,1280]{3,2,1,0:T(8,128)(2,1)}, u32[]{:S(2)}) copy-start(bf16[1,1,128,1280]{3,2,1,0:T(8,128)(2,1)} %param.12) | copy-start | bytes 983044
  6.5 38.6 %all-gather.5.cloned.1.call-start = ((), (), s32[]{:S(2)}) async-start(), calls=%async_computation.5 | async-start | bytes 1638400 | tf_op jit(solution)/shard_map/all_gather | solution.py:78
  8.5 69.4 %all-gather.7.cloned.1.call-start = ((), (), s32[]{:S(2)}) async-start(), calls=%async_computation.6 | async-start | bytes 1638400 | tf_op jit(solution)/shard_map/all_gather | solution.py:79
  9.2 126.8 %reduce-scatter.2.cloned.1.call-start = ((), (), s32[]{:S(2)}) async-start(), calls=%async_computation.4 | async-start | bytes 3932160 | tf_op jit(solution)/shard_map/reduce_scatter | solution.py:100
  99.3 0.7 copy-start.5
  99.3 0.7 copy-start.6
  99.3 0.8 copy-start.7
  99.3 36.8 %copy-start.2 = (bf16[1,1,128,2560]{3,2,1,0:T(8,128)(2,1)S(1)}, bf16[1,1,128,2560]{3,2,1,0:T(8,128)(2,1)}, u32[]{:S(2)}) copy-start(bf16[1,1,128,2560]{3,2,1,0:T(8,128)(2,1)} %param.15) | copy-start | bytes 1966084
  136.0 6.7 %copy-start.1 = (f32[128,2560]{1,0:T(8,128)S(1)}, f32[128,2560]{1,0:T(8,128)}, u32[]{:S(2)}) copy-start(f32[128,2560]{1,0:T(8,128)} %reduce-scatter.2.cloned.1.call-done) | copy-start | bytes 3932164
  142.8 8.8 %copy-start.8 = (s32[1,4]{1,0:T(1,128)S(1)}, s32[1,4]{1,0:T(1,128)}, u32[]{:S(2)}) copy-start(s32[1,4]{1,0:T(1,128)} %param.23) | copy-start | bytes 52
  142.8 25.6 %copy-start.4 = (f32[1,1,128,32]{2,3,1,0:T(8,128)S(1)}, f32[1,1,128,32]{2,3,1,0:T(8,128)}, u32[]{:S(2)}) copy-start(f32[1,1,128,32]{2,3,1,0:T(8,128)} %param.21) | copy-start | bytes 49156
  152.6 10.7 %all-to-all-start.1 = ((f32[4,1,2048]{2,1,0:T(1,128)}), f32[4,1,2048]{2,1,0:T(1,128)S(1)}, u32[]{:S(2)}, u32[]{:S(2)}) async-start(f32[4,1,2048]{2,1,0:T(1,128)} %reshape.232), calls=%async_computation.2 | async-start | bytes 65536 | tf_op jit(solution)/shard_map/all_to_all | solution.py:129
Sparse Core Ops, SparseCore 0:
  8.9 36.1 all-gather.4
  46.7 31.2 all-gather.6
  99.4 36.5 reduce-scatter.1
where the time goes:
time: 176 us
  waiting for transfers between devices  108 us (61%)
  blocking collectives  24.5 us (14%)
  between operations  14 us (8%)
  local copies, waits for them, and re-layouts  10.7 us (6%)
  matrix products  10.1 us (6%)
  starting transfers between devices  5.08 us (3%)
  other arithmetic  3.65 us (2%)
    reduce_scatter x1, waiting for transfers between devices, on_device(): lax.psum_scatter(projected, 'shard', scatter_dimension=1, tiled=True)  35.9 us
    all_gather x1, waiting for transfers between devices, on_device(): lax.all_gather(key_vecs[0], 'seq', axis=1, tiled=True)  35.6 us
    all_gather x1, waiting for transfers between devices, on_device(): lax.all_gather(value_vecs[0], 'seq', axis=1, tiled=True)  30.4 us
    psum x1, blocking collectives, on_device(): predicted = lax.psum(partial_head, 'shard')  7.66 us
    all_to_all x1, blocking collectives, on_device(): lax.all_to_all(both_rows.reshape(2, row_count, half_width), 'guide', spli...  5.84 us
    unnamed x23, local copies, waits for them, and re-layouts  5.6 us
    all_to_all x1, starting transfers between devices, on_device(): lax.all_to_all(by_owner[None], 'seq', split_axis=2, concat_axis=3, tiled=...  4.99 us
    all_to_all x1, waiting for transfers between devices, on_device(): lax.all_to_all(by_owner[None], 'seq', split_axis=2, concat_axis=3, tiled=...  4.96 us
  transfers between devices with their start and end apart: 4, of which 4 were waited for; matrix products, arithmetic and copies ran while one was open for 2% of the time, Pallas kernels for 0%

commit v1 on v0

v1 whole, which is shorter than its diff:
```python
import functools
import math

import jax
import jax.numpy as jnp
from jax import lax
from jax.experimental import pallas as pl
from jax.experimental.pallas import tpu as pltpu
from jax.sharding import PartitionSpec as P

HEAD_DIM = 128
MESH = pl.DeviceIdType.MESH

beta_low = 0.0001
beta_high = 0.02
guidance_scale = 3.0
norm_epsilon = 1e-06


def plan_weight(timesteps):
    steps_float = timesteps.astype(jnp.float32)
    exponent = (steps_float + 1.0) * beta_low + (beta_high - beta_low) * steps_float * (
        steps_float + 1.0
    ) / (2.0 * 999.0)
    return 1.0 - jnp.exp(-exponent)


def attend(q, k, v):
    scores = lax.dot_general(q, k, (((1,), (1,)), ((), ())), preferred_element_type=jnp.float32)
    top = jnp.max(scores, axis=-1, keepdims=True)
    expo = jnp.exp2((scores - top) * (HEAD_DIM ** (-0.5) * math.log2(math.e)))
    denom = jnp.sum(expo, axis=-1, keepdims=True)
    mixed = jnp.dot(expo.astype(jnp.bfloat16), v, preferred_element_type=jnp.float32)
    return (mixed / denom).astype(jnp.bfloat16)


def kernel(
    n_seq, n_shard, width_all, chunk,
    q_hbm, k_hbm, v_hbm, res_hbm, w_hbm, gate_hbm, shift_hbm, scale_hbm, wh_hbm, noise_hbm,
    steps_ref, owner_ref, out_ref,
    qkv, left, q_left, att, ostage, w_vm, res_vm, vec_vm, wh_vm, noise_vm,
    psend, pbuf, msg, gbuf, fsend,
    z_send, z_recv, l_send, l_recv, o_send, o_recv, a_send, a_recv,
    p_send, p_recv, m_send, m_recv, f_send, f_recv, in_sem, own_sem,
):
    z, s, g = lax.axis_index("seq"), lax.axis_index("shard"), lax.axis_index("guide")
    rows, width = q_hbm.shape
    heads = width // HEAD_DIM
    n_full = heads // n_seq
    n_left = heads - n_full * n_seq
    left_at = n_full * n_seq * HEAD_DIM
    half = w_hbm.shape[1]
    feats = res_hbm.shape[1]
    per = half // feats
    n_chunk = feats // chunk
    channels = wh_hbm.shape[1]
    n_frame = owner_ref.shape[1]
    frame_rows = rows // n_frame

    def head_cols(index):
        return pl.ds(pl.multiple_of(index * HEAD_DIM, HEAD_DIM), HEAD_DIM)

    def block_rows(index):
        return pl.ds(pl.multiple_of(index * rows, rows), rows)

    def ahead(d):
        return lax.rem(z + d, n_seq)

    def behind(d):
        return lax.rem(z + n_seq - d, n_seq)

    own = []
    tensors = (q_hbm, k_hbm, v_hbm)
    for a in range(n_full):
        for t in range(3):
            own.append(pltpu.make_async_copy(
                tensors[t].at[:, head_cols(z * n_full + a)], qkv.at[a, t, block_rows(z)],
                own_sem.at[a * 3 + t]))
    if n_left:
        for t in range(2):
            own.append(pltpu.make_async_copy(
                tensors[t + 1].at[:, pl.ds(left_at, n_left * HEAD_DIM)], left.at[t, block_rows(z)],
                own_sem.at[n_full * 3 + t]))
        own.append(pltpu.make_async_copy(
            q_hbm.at[:, pl.ds(left_at, n_left * HEAD_DIM)], q_left, own_sem.at[n_full * 3 + 2]))
    loads = [
        pltpu.make_async_copy(gate_hbm, vec_vm.at[0], in_sem.at[0]),
        pltpu.make_async_copy(shift_hbm, vec_vm.at[1], in_sem.at[1]),
        pltpu.make_async_copy(scale_hbm, vec_vm.at[2], in_sem.at[2]),
        pltpu.make_async_copy(wh_hbm, wh_vm, in_sem.at[3]),
        pltpu.make_async_copy(noise_hbm, noise_vm, in_sem.at[4]),
        pltpu.make_async_copy(res_hbm, res_vm, in_sem.at[5]),
        pltpu.make_async_copy(w_hbm, w_vm, in_sem.at[6]),
    ]

    barrier = pltpu.get_barrier_semaphore()
    for d in range(1, n_seq):
        pl.semaphore_signal(barrier, inc=1, device_id={"seq": ahead(d)}, device_id_type=MESH)
    n_local = 2 * n_shard
    me_local = s * 2 + g

    def local_peer(d):
        index = lax.rem(me_local + d, n_local)
        return {"shard": index // 2, "guide": index % 2}

    for d in range(1, n_local):
        pl.semaphore_signal(barrier, inc=1, device_id=local_peer(d), device_id_type=MESH)
    for copy in own:
        copy.start()
    pl.semaphore_wait(barrier, n_seq - 1 + n_local - 1)

    order = sorted(range(1, n_seq), key=lambda d: -min(d, n_seq - d))
    z_copies = {}
    for a in range(n_full):
        for d in order:
            for t in range(3):
                copy = pltpu.make_async_remote_copy(
                    src_ref=tensors[t].at[:, head_cols(ahead(d) * n_full + a)],
                    dst_ref=qkv.at[a, t, block_rows(z)],
                    send_sem=z_send.at[a, t, d - 1], recv_sem=z_recv.at[a, t, d - 1],
                    device_id={"seq": ahead(d)}, device_id_type=MESH)
                copy.start()
                z_copies[a, d, t] = copy
    l_copies = []
    if n_left:
        for d in order:
            for t in range(2):
                copy = pltpu.make_async_remote_copy(
                    src_ref=tensors[t + 1].at[:, pl.ds(left_at, n_left * HEAD_DIM)],
                    dst_ref=left.at[t, block_rows(z)],
                    send_sem=l_send.at[t, d - 1], recv_sem=l_recv.at[t, d - 1],
                    device_id={"seq": ahead(d)}, device_id_type=MESH)
                copy.start()
                l_copies.append(copy)
    for copy in loads:
        copy.start()

    for copy in loads[:6]:
        copy.wait()
    gains = jnp.concatenate([1.0 + vec_vm[2], vec_vm[1]], axis=0)
    consts = jnp.dot(
        gains, wh_vm[...].astype(jnp.float32),
        precision=lax.Precision.HIGHEST, preferred_element_type=jnp.float32)
    msg[me_local, rows:, :] = jnp.zeros((8, msg.shape[2]), jnp.float32)
    msg[me_local, rows : rows + 2, 0:channels] = consts
    for copy in own:
        copy.wait()

    o_copies = []
    for a in range(n_full):
        for d in range(1, n_seq):
            for t in range(3):
                z_copies[a, d, t].wait_recv()
        for d in order + [0]:
            to = ahead(d)
            mixed = attend(qkv[a, 0, block_rows(to)], qkv[a, 1], qkv[a, 2])
            cols = head_cols(z * n_full + a)
            if d == 0:
                att[g, :, cols] = mixed
            else:
                ostage[a, d - 1] = mixed
                copy = pltpu.make_async_remote_copy(
                    src_ref=ostage.at[a, d - 1], dst_ref=att.at[g, :, cols],
                    send_sem=o_send.at[a, d - 1], recv_sem=o_recv.at[a, d - 1],
                    device_id={"seq": to}, device_id_type=MESH)
                copy.start()
                o_copies.append(copy)
    for copy in l_copies:
        copy.wait_recv()
    for h in range(n_left):
        cols = pl.ds(h * HEAD_DIM, HEAD_DIM)
        att[g, :, pl.ds(left_at + h * HEAD_DIM, HEAD_DIM)] = attend(
            q_left[:, cols], left[0, :, cols], left[1, :, cols])
    for a in range(n_full):
        for d in range(1, n_seq):
            pltpu.make_async_remote_copy(
                src_ref=ostage.at[a, d - 1], dst_ref=att.at[g, :, head_cols(behind(d) * n_full + a)],
                send_sem=o_send.at[a, d - 1], recv_sem=o_recv.at[a, d - 1],
                device_id={"seq": ahead(d)}, device_id_type=MESH).wait_recv()

    swap = pltpu.make_async_remote_copy(
        src_ref=att.at[g], dst_ref=att.at[g], send_sem=a_send, recv_sem=a_recv,
        device_id={"guide": 1 - g}, device_id_type=MESH)
    swap.start()
    loads[6].wait()
    swap.wait_recv()

    def p_copy(b, q, c):
        return pltpu.make_async_remote_copy(
            src_ref=psend.at[b, q, c], dst_ref=pbuf.at[s, c],
            send_sem=p_send.at[b, q, c], recv_sem=p_recv.at[s, c],
            device_id={"shard": g * per + q, "guide": b}, device_id_type=MESH)

    def is_me(b, q):
        return jnp.logical_and(g == b, g * per + q == s)

    both = jnp.concatenate([att[0], att[1]], axis=0)
    for c in range(n_chunk):
        for q in range(per):
            part = jnp.dot(
                both, w_vm[:, q * feats + c * chunk : q * feats + (c + 1) * chunk],
                preferred_element_type=jnp.float32).astype(jnp.bfloat16)
            for b in range(2):
                psend[b, q, c] = part[b * rows : (b + 1) * rows]

                @pl.when(is_me(b, q))
                def _():
                    pbuf[s, c] = psend[b, q, c]

                @pl.when(jnp.logical_not(is_me(b, q)))
                def _():
                    p_copy(b, q, c).start()

    from_guide = s // per
    first = jnp.zeros((rows, 1), jnp.float32)
    second = jnp.zeros((rows, 1), jnp.float32)
    head = jnp.zeros((rows, channels), jnp.float32)
    for c in range(n_chunk):
        for r in range(n_shard):

            @pl.when(jnp.logical_not(jnp.logical_and(from_guide == g, s == r)))
            def _():
                pltpu.make_async_remote_copy(
                    src_ref=psend.at[0, 0, c], dst_ref=pbuf.at[r, c],
                    send_sem=p_send.at[0, 0, c], recv_sem=p_recv.at[r, c],
                    device_id={"guide": 1 - g}, device_id_type=MESH).wait_recv()

        at = slice(c * chunk, (c + 1) * chunk)
        total = pbuf[0, c].astype(jnp.float32)
        for r in range(1, n_shard):
            total = total + pbuf[r, c].astype(jnp.float32)
        hidden = res_vm[:, at].astype(jnp.float32) + vec_vm[0, :, at] * total
        first = first + jnp.sum(hidden, axis=-1, keepdims=True)
        second = second + jnp.sum(hidden * hidden, axis=-1, keepdims=True)
        gained = hidden * (1.0 + vec_vm[2, :, at])
        high = gained.astype(jnp.bfloat16)
        rest = gained - high.astype(jnp.float32)
        low = rest.astype(jnp.bfloat16)
        last = (rest - low.astype(jnp.float32)).astype(jnp.bfloat16)
        wh = wh_vm[c * chunk : (c + 1) * chunk, :]
        for piece in (last, low, high):
            head = head + jnp.dot(piece, wh, preferred_element_type=jnp.float32)
    msg[me_local, 0:rows, 0:channels] = head
    tail = msg.shape[2] - channels
    lane = lax.broadcasted_iota(jnp.int32, (rows, tail), 1)
    msg[me_local, 0:rows, channels:] = jnp.where(lane == 0, first, second)
    m_copies = []
    for d in range(1, n_local):
        copy = pltpu.make_async_remote_copy(
            src_ref=msg.at[me_local], dst_ref=msg.at[me_local],
            send_sem=m_send.at[d - 1], recv_sem=m_recv.at[d - 1],
            device_id=local_peer(d), device_id_type=MESH)
        copy.start()
        m_copies.append(copy)
    for copy in m_copies:
        copy.wait_recv()

    eps = []
    for b in range(2):
        total = msg[b]
        for r in range(1, n_shard):
            total = total + msg[r * 2 + b]
        mean = total[0:rows, channels : channels + 1] / width_all
        var = total[0:rows, channels + 1 : channels + 2] / width_all - mean * mean
        inv = lax.rsqrt(var + norm_epsilon)
        eps.append(
            (total[0:rows, 0:channels] - mean * total[rows : rows + 1, 0:channels]) * inv
            + total[rows + 1 : rows + 2, 0:channels])
    guided = eps[1] + guidance_scale * (eps[0] - eps[1])

    f_copies = []
    for d in order + [0]:
        to = ahead(d)
        picked = jnp.zeros((frame_rows, channels), jnp.float32)
        for f in range(n_frame):
            hit = jnp.full((1, channels), owner_ref[0, f], jnp.int32) == to
            picked = picked + jnp.where(hit, guided[f * frame_rows : (f + 1) * frame_rows], 0.0)
        if d == 0:
            gbuf[z] = picked
        else:
            fsend[d - 1] = picked
            copy = pltpu.make_async_remote_copy(
                src_ref=fsend.at[d - 1], dst_ref=gbuf.at[z],
                send_sem=f_send.at[d - 1], recv_sem=f_recv.at[d - 1],
                device_id={"seq": to}, device_id_type=MESH)
            copy.start()
            f_copies.append(copy)
    out_ch = channels // 2
    weight = plan_weight(jnp.full((1, out_ch), steps_ref[0], jnp.int32))
    for copy in f_copies:
        copy.wait_recv()
    is_first = jnp.full((1, out_ch), g, jnp.int32) == 0
    for r in range(n_seq):
        rows_r = slice(r * frame_rows, (r + 1) * frame_rows)
        mine = jnp.where(is_first, gbuf[r, :, 0:out_ch], gbuf[r, :, out_ch:])
        out_ref[rows_r, :] = weight * (mine - noise_vm[rows_r, :])

    for copy in list(z_copies.values()) + l_copies + o_copies + m_copies + f_copies + [swap]:
        copy.wait_send()
    for c in range(n_chunk):
        for q in range(per):
            for b in range(2):

                @pl.when(jnp.logical_not(is_me(b, q)))
                def _():
                    p_copy(b, q, c).wait_send()


def on_device(
    n_seq, n_shard,
    queries, key_vecs, value_vecs, residual, w_out, attn_gate, norm_shift, norm_scale, w_head,
    noise, timesteps, frame_owner,
):
    rows, width = queries.shape[2:]
    heads = width // HEAD_DIM
    n_full = heads // n_seq
    n_left = heads - n_full * n_seq
    half = w_out.shape[1]
    feats = residual.shape[3]
    per = half // feats
    chunk = next(size for size in (512, 256, 128) if feats % size == 0)
    n_chunk = feats // chunk
    channels = w_head.shape[1]
    n_frame = frame_owner.shape[1]
    frame_rows = rows // n_frame
    n_local = 2 * n_shard
    bf16, f32 = jnp.bfloat16, jnp.float32
    full1, left1 = max(n_full, 1), max(n_left, 1)
    dma = pltpu.SemaphoreType.DMA
    hbm = pl.BlockSpec(memory_space=pl.ANY)
    smem = pl.BlockSpec(memory_space=pltpu.SMEM)
    out = pl.pallas_call(
        functools.partial(kernel, n_seq, n_shard, feats * n_shard, chunk),
        out_shape=jax.ShapeDtypeStruct(noise.shape[2:], f32),
        in_specs=[hbm] * 10 + [smem, smem],
        out_specs=pl.BlockSpec(memory_space=pltpu.VMEM),
        scratch_shapes=[
            pltpu.VMEM((full1, 3, n_seq * rows, HEAD_DIM), bf16),
            pltpu.VMEM((2, n_seq * rows, left1 * HEAD_DIM), bf16),
            pltpu.VMEM((rows, left1 * HEAD_DIM), bf16),
            pltpu.VMEM((2, rows, width), bf16),
            pltpu.VMEM((full1, n_seq - 1, rows, HEAD_DIM), bf16),
            pltpu.VMEM(w_out.shape, bf16),
            pltpu.VMEM((rows, feats), bf16),
            pltpu.VMEM((3, 1, feats), f32),
            pltpu.VMEM(w_head.shape, bf16),
            pltpu.VMEM(noise.shape[2:], f32),
            pltpu.VMEM((2, per, n_chunk, rows, chunk), bf16),
            pltpu.VMEM((n_shard, n_chunk, rows, chunk), bf16),
            pltpu.VMEM((n_local, rows + 8, 128), f32),
            pltpu.VMEM((n_seq, frame_rows, channels), f32),
            pltpu.VMEM((n_seq - 1, frame_rows, channels), f32),
            dma((full1, 3, n_seq - 1)), dma((full1, 3, n_seq - 1)),
            dma((2, n_seq - 1)), dma((2, n_seq - 1)),
            dma((full1, n_seq - 1)), dma((full1, n_seq - 1)),
            dma, dma,
            dma((2, per, n_chunk)), dma((n_shard, n_chunk)),
            dma((n_local - 1,)), dma((n_local - 1,)),
            dma((n_seq - 1,)), dma((n_seq - 1,)),
            dma((7,)), dma((n_full * 3 + 3,)),
        ],
        compiler_params=pltpu.CompilerParams(
            collective_id=0, has_side_effects=True, vmem_limit_bytes=48 * 1024 * 1024),
    )(
        queries[0, 0], key_vecs[0, 0], value_vecs[0, 0], residual[0, 0], w_out,
        attn_gate, norm_shift, norm_scale, w_head, noise[0, 0], timesteps, frame_owner,
    )
    return out[None, None]


def solution(mesh):
    return jax.shard_map(
        functools.partial(on_device, mesh.shape["seq"], mesh.shape["shard"]),
        mesh=mesh,
        in_specs=(
            P("guide", "group", "seq", "shard"),
            P("guide", "group", "seq", "shard"),
            P("guide", "group", "seq", "shard"),
            P("guide", "group", "seq", "shard"),
            P("shard", "guide"),
            P("group", "shard"),
            P("group", "shard"),
            P("group", "shard"),
            P("shard", None),
            P("group", "seq", None, "guide"),
            P("group"),
            P("group", None),
        ),
        out_specs=P("group", "seq", None, "guide"),
        check_vma=False,
    )
```

time: 176 us -> 78.1 us (0.44)
  waiting for transfers between devices: 108 us -> 0 us
  Pallas kernels: 0 us -> 67.3 us
  blocking collectives: 24.5 us -> 0 us
  between operations: 14 us -> 0.68 us
  matrix products: 10.1 us -> 0 us
  starting transfers between devices: 5.08 us -> 0 us
  other arithmetic: 3.65 us -> 0 us
    pallas_call x0 -> x1, Pallas kernels: none -> 67.3 us  [on_device(): pl.pallas_call(functools.partial(kernel, n_seq, n_shard, feats * n_shard,...]
    all_gather x2 -> x0, waiting for transfers between devices: 66 us -> none  [the longest x1 35.6 us: on_device(): lax.all_gather(key_vecs[0], 'seq', axis=1, tiled=True)]
    reduce_scatter x1 -> x0, waiting for transfers between devices: 35.9 us -> none  [on_device(): lax.psum_scatter(projected, 'shard', scatter_dimension=1, tiled=True)]
    psum x2 -> x0, blocking collectives: 12.6 us -> none  [the longest x1 7.66 us: on_device(): predicted = lax.psum(partial_head, 'shard')]
    dot_general x5 -> x0, matrix products: 10.1 us -> none  [the longest x1 4.74 us: on_device(): jnp.dot(lax.all_gather(attended, 'guide', axis=0, tiled=True), w_out, pre...]
    all_to_all x2 -> x0, blocking collectives: 9.6 us -> none  [the longest x1 5.84 us: on_device(): lax.all_to_all(both_rows.reshape(2, row_count, half_width), 'guide', spli...]
    all_to_all x1 -> x0, starting transfers between devices: 4.99 us -> none  [on_device(): lax.all_to_all(by_owner[None], 'seq', split_axis=2, concat_axis=3, tiled=...]
    all_to_all x1 -> x0, waiting for transfers between devices: 4.96 us -> none  [on_device(): lax.all_to_all(by_owner[None], 'seq', split_axis=2, concat_axis=3, tiled=...]
  transfers between devices with their start and end apart: 4 -> 0, of which waited for: 4 -> 0; matrix products, arithmetic and copies ran while one was open for 2% -> 0% of each run, Pallas kernels for 0% -> 0%
where the time goes in v1:
time: 78.1 us; the launch traced here: 77.6 us
  Pallas kernels  67.3 us (86%)
  local copies, waits for them, and re-layouts  9.55 us (12%)
    pallas_call x1, Pallas kernels, on_device(): pl.pallas_call(functools.partial(kernel, n_seq, n_shard, feats * n_shard,...  67.3 us
    unnamed x18, local copies, waits for them, and re-layouts  8.87 us

profile of v1, /device:TPU:0, one launch (start us, length us, event | category | flops | bytes accessed | tf_op | source)
XLA Modules:
  0.0 77.6 jit_solution(3981716301426196590)
XLA Ops:
  0.7 0.8 %copy.13 = f32[1,1,128,32]{3,2,1,0:T(8,128)S(1)} copy(f32[1,1,128,32]{2,3,1,0:T(8,128)} %param.21) | data formatting | bytes 32768 | tf_op args[9]
  1.5 1.3 %copy.14.wh_hbm = bf16[2560,64]{1,0:T(8,128)(2,1)S(1)} copy(bf16[2560,64]{0,1:T(8,128)(2,1)} %param.20) | data formatting | bytes 655360 | tf_op args[8]
  2.8 0.0 copy-start
  2.8 1.1 %copy-done = bf16[1,1,128,2560]{3,2,1,0:T(8,128)(2,1)S(1)} copy-done((bf16[1,1,128,2560]{3,2,1,0:T(8,128)(2,1)S(1)}, bf16[1,1,128,2560]{3,2,1,0:T(8,128)(2,1)}, u32[]{:S(2)}) %copy-start) | copy-done | bytes 655384
  3.9 0.0 copy-start.1
  3.9 1.0 %copy-done.1 = bf16[1,1,128,1280]{3,2,1,0:T(8,128)(2,1)S(1)} copy-done((bf16[1,1,128,1280]{3,2,1,0:T(8,128)(2,1)S(1)}, bf16[1,1,128,1280]{3,2,1,0:T(8,128)(2,1)}, u32[]{:S(2)}) %copy-start.1) | copy-done | bytes 327704
  4.8 0.0 copy-start.2
  4.8 1.0 %copy-done.2 = bf16[1,1,128,1280]{3,2,1,0:T(8,128)(2,1)S(1)} copy-done((bf16[1,1,128,1280]{3,2,1,0:T(8,128)(2,1)S(1)}, bf16[1,1,128,1280]{3,2,1,0:T(8,128)(2,1)}, u32[]{:S(2)}) %copy-start.2) | copy-done | bytes 327704
  5.8 0.0 copy-start.3
  5.8 1.0 %copy-done.3 = bf16[1,1,128,1280]{3,2,1,0:T(8,128)(2,1)S(1)} copy-done((bf16[1,1,128,1280]{3,2,1,0:T(8,128)(2,1)S(1)}, bf16[1,1,128,1280]{3,2,1,0:T(8,128)(2,1)}, u32[]{:S(2)}) %copy-start.3) | copy-done | bytes 327704
  6.8 0.0 copy-start.4
  6.8 0.7 copy-done.4
  7.5 0.0 copy-start.5
  7.5 0.7 copy-done.5
  8.2 0.0 copy-start.6
  8.2 0.7 copy-done.6
  8.9 0.0 copy-start.7
  8.9 0.7 copy-done.7
  9.5 67.3 %shard_map.118 = f32[128,32]{1,0:T(8,128)S(1)} custom-call(bf16[128,1280]{1,0:T(8,128)(2,1)S(1)} %bitcast.7, bf16[128,1280]{1,0:T(8,128)(2,1)S(1)} %bitcast.8, bf16[128,1280]{1,0:T(8,128)(2,1)S(1)} %bitcast.9, bf16[128,2560]{1,0:T(8,128)(2,1)S(1)} %bitcast.6, bf16[1280,2560]{1,0:T(8,128)(2,1)} %w_hbm.1, f32[1,2560]{1,0:T(1,128)S(1)} %copy-done.4, ...), custom_call_target="tpu_custom_call" | custom-call | tf_op jit(solution)/shard_map/pallas_call | solution.py:332
  76.9 0.7 copy.15
Async XLA Ops:
  2.8 1.1 %copy-start = (bf16[1,1,128,2560]{3,2,1,0:T(8,128)(2,1)S(1)}, bf16[1,1,128,2560]{3,2,1,0:T(8,128)(2,1)}, u32[]{:S(2)}) copy-start(bf16[1,1,128,2560]{3,2,1,0:T(8,128)(2,1)} %param.15) | copy-start | bytes 1966084
  3.9 1.0 %copy-start.1 = (bf16[1,1,128,1280]{3,2,1,0:T(8,128)(2,1)S(1)}, bf16[1,1,128,1280]{3,2,1,0:T(8,128)(2,1)}, u32[]{:S(2)}) copy-start(bf16[1,1,128,1280]{3,2,1,0:T(8,128)(2,1)} %param.12) | copy-start | bytes 983044
  4.8 1.0 %copy-start.2 = (bf16[1,1,128,1280]{3,2,1,0:T(8,128)(2,1)S(1)}, bf16[1,1,128,1280]{3,2,1,0:T(8,128)(2,1)}, u32[]{:S(2)}) copy-start(bf16[1,1,128,1280]{3,2,1,0:T(8,128)(2,1)} %param.13) | copy-start | bytes 983044
  5.8 1.0 %copy-start.3 = (bf16[1,1,128,1280]{3,2,1,0:T(8,128)(2,1)S(1)}, bf16[1,1,128,1280]{3,2,1,0:T(8,128)(2,1)}, u32[]{:S(2)}) copy-start(bf16[1,1,128,1280]{3,2,1,0:T(8,128)(2,1)} %param.14) | copy-start | bytes 983044
  6.8 0.7 copy-start.4
  7.5 0.7 copy-start.5
  8.2 0.7 copy-start.6
  8.9 0.7 copy-start.7

commit v2 on v1

--- a/solution.py
+++ b/solution.py
@@ -37,8 +37,8 @@
 def kernel(
     n_seq, n_shard, width_all, chunk,
     q_hbm, k_hbm, v_hbm, res_hbm, w_hbm, gate_hbm, shift_hbm, scale_hbm, wh_hbm, noise_hbm,
-    steps_ref, owner_ref, out_ref,
-    qkv, left, q_left, att, ostage, w_vm, res_vm, vec_vm, wh_vm, noise_vm,
+    steps_hbm, owner_hbm, out_ref,
+    qkv, left, q_left, att, ostage, w_vm, res_vm, vec_vm, wh_vm, noise_vm, steps_vm, owner_vm,
     psend, pbuf, msg, gbuf, fsend,
     z_send, z_recv, l_send, l_recv, o_send, o_recv, a_send, a_recv,
     p_send, p_recv, m_send, m_recv, f_send, f_recv, in_sem, own_sem,
@@ -53,8 +53,8 @@
     feats = res_hbm.shape[1]
     per = half // feats
     n_chunk = feats // chunk
-    channels = wh_hbm.shape[1]
-    n_frame = owner_ref.shape[1]
+    channels = wh_hbm.shape[0]
+    n_frame = owner_hbm.shape[1]
     frame_rows = rows // n_frame
 
     def head_cols(index):
@@ -90,7 +90,9 @@
         pltpu.make_async_copy(wh_hbm, wh_vm, in_sem.at[3]),
         pltpu.make_async_copy(noise_hbm, noise_vm, in_sem.at[4]),
         pltpu.make_async_copy(res_hbm, res_vm, in_sem.at[5]),
-        pltpu.make_async_copy(w_hbm, w_vm, in_sem.at[6]),
+        pltpu.make_async_copy(steps_hbm, steps_vm, in_sem.at[6]),
+        pltpu.make_async_copy(owner_hbm, owner_vm, in_sem.at[7]),
+        pltpu.make_async_copy(w_hbm, w_vm, in_sem.at[8]),
     ]
 
     barrier = pltpu.get_barrier_semaphore()
@@ -135,11 +137,11 @@
     for copy in loads:
         copy.start()
 
-    for copy in loads[:6]:
+    for copy in loads[:8]:
         copy.wait()
     gains = jnp.concatenate([1.0 + vec_vm[2], vec_vm[1]], axis=0)
-    consts = jnp.dot(
-        gains, wh_vm[...].astype(jnp.float32),
+    consts = lax.dot_general(
+        gains, wh_vm[...].astype(jnp.float32), (((1,), (1,)), ((), ())),
         precision=lax.Precision.HIGHEST, preferred_element_type=jnp.float32)
     msg[me_local, rows:, :] = jnp.zeros((8, msg.shape[2]), jnp.float32)
     msg[me_local, rows : rows + 2, 0:channels] = consts
@@ -182,7 +184,7 @@
         src_ref=att.at[g], dst_ref=att.at[g], send_sem=a_send, recv_sem=a_recv,
         device_id={"guide": 1 - g}, device_id_type=MESH)
     swap.start()
-    loads[6].wait()
+    loads[8].wait()
     swap.wait_recv()
 
     def p_copy(b, q, c):
@@ -237,9 +239,10 @@
         rest = gained - high.astype(jnp.float32)
         low = rest.astype(jnp.bfloat16)
         last = (rest - low.astype(jnp.float32)).astype(jnp.bfloat16)
-        wh = wh_vm[c * chunk : (c + 1) * chunk, :]
+        wh = wh_vm[:, at]
         for piece in (last, low, high):
-            head = head + jnp.dot(piece, wh, preferred_element_type=jnp.float32)
+            head = head + lax.dot_general(
+                piece, wh, (((1,), (1,)), ((), ())), preferred_element_type=jnp.float32)
     msg[me_local, 0:rows, 0:channels] = head
     tail = msg.shape[2] - channels
     lane = lax.broadcasted_iota(jnp.int32, (rows, tail), 1)
@@ -273,7 +276,7 @@
         to = ahead(d)
         picked = jnp.zeros((frame_rows, channels), jnp.float32)
         for f in range(n_frame):
-            hit = jnp.full((1, channels), owner_ref[0, f], jnp.int32) == to
+            hit = owner_vm[:, f : f + 1] == to
             picked = picked + jnp.where(hit, guided[f * frame_rows : (f + 1) * frame_rows], 0.0)
         if d == 0:
             gbuf[z] = picked
@@ -286,14 +289,13 @@
             copy.start()
             f_copies.append(copy)
     out_ch = channels // 2
-    weight = plan_weight(jnp.full((1, out_ch), steps_ref[0], jnp.int32))
+    weight = plan_weight(jnp.full((1, rows), steps_vm[0], jnp.int32))
     for copy in f_copies:
         copy.wait_recv()
-    is_first = jnp.full((1, out_ch), g, jnp.int32) == 0
-    for r in range(n_seq):
-        rows_r = slice(r * frame_rows, (r + 1) * frame_rows)
-        mine = jnp.where(is_first, gbuf[r, :, 0:out_ch], gbuf[r, :, out_ch:])
-        out_ref[rows_r, :] = weight * (mine - noise_vm[rows_r, :])
+    frame = gbuf[...].reshape(n_seq * frame_rows, channels).T
+    is_first = jnp.full((out_ch, 1), g, jnp.int32) == 0
+    mine = jnp.where(is_first, frame[0:out_ch], frame[out_ch:])
+    out_ref[...] = weight * (mine - noise_vm[...])
 
     for copy in list(z_copies.values()) + l_copies + o_copies + m_copies + f_copies + [swap]:
         copy.wait_send()
@@ -323,16 +325,16 @@
     channels = w_head.shape[1]
     n_frame = frame_owner.shape[1]
     frame_rows = rows // n_frame
+    noise_t = noise[0, 0].T
     n_local = 2 * n_shard
     bf16, f32 = jnp.bfloat16, jnp.float32
     full1, left1 = max(n_full, 1), max(n_left, 1)
     dma = pltpu.SemaphoreType.DMA
-    hbm = pl.BlockSpec(memory_space=pl.ANY)
-    smem = pl.BlockSpec(memory_space=pltpu.SMEM)
+    hbm = pl.BlockSpec(memory_space=pltpu.HBM)
     out = pl.pallas_call(
         functools.partial(kernel, n_seq, n_shard, feats * n_shard, chunk),
-        out_shape=jax.ShapeDtypeStruct(noise.shape[2:], f32),
-        in_specs=[hbm] * 10 + [smem, smem],
+        out_shape=jax.ShapeDtypeStruct(noise_t.shape, f32),
+        in_specs=[hbm] * 12,
         out_specs=pl.BlockSpec(memory_space=pltpu.VMEM),
         scratch_shapes=[
             pltpu.VMEM((full1, 3, n_seq * rows, HEAD_DIM), bf16),
@@ -343,8 +345,10 @@
             pltpu.VMEM(w_out.shape, bf16),
             pltpu.VMEM((rows, feats), bf16),
             pltpu.VMEM((3, 1, feats), f32),
-            pltpu.VMEM(w_head.shape, bf16),
-            pltpu.VMEM(noise.shape[2:], f32),
+            pltpu.VMEM((channels, feats), bf16),
+            pltpu.VMEM(noise_t.shape, f32),
+            pltpu.SMEM((1,), jnp.int32),
+            pltpu.VMEM((1, n_frame), jnp.int32),
             pltpu.VMEM((2, per, n_chunk, rows, chunk), bf16),
             pltpu.VMEM((n_shard, n_chunk, rows, chunk), bf16),
             pltpu.VMEM((n_local, rows + 8, 128), f32),
@@ -357,15 +361,15 @@
             dma((2, per, n_chunk)), dma((n_shard, n_chunk)),
             dma((n_local - 1,)), dma((n_local - 1,)),
             dma((n_seq - 1,)), dma((n_seq - 1,)),
-            dma((7,)), dma((n_full * 3 + 3,)),
+            dma((9,)), dma((n_full * 3 + 3,)),
         ],
         compiler_params=pltpu.CompilerParams(
-            collective_id=0, has_side_effects=True, vmem_limit_bytes=48 * 1024 * 1024),
+            collective_id=0, has_side_effects=True, vmem_limit_bytes=63 * 1024 * 1024),
     )(
         queries[0, 0], key_vecs[0, 0], value_vecs[0, 0], residual[0, 0], w_out,
-        attn_gate, norm_shift, norm_scale, w_head, noise[0, 0], timesteps, frame_owner,
+        attn_gate, norm_shift, norm_scale, w_head.T, noise_t, timesteps, frame_owner,
     )
-    return out[None, None]
+    return out.T[None, None]
 
 
 def solution(mesh):

time: 78.1 us -> 70.2 us (0.90)
  local copies, waits for them, and re-layouts: 9.55 us -> 1.32 us
    unnamed x18 -> x1, local copies, waits for them, and re-layouts: 8.87 us -> 1.32 us
where the time goes in v2:
time: 70.2 us; the launch traced here: 69.9 us
  Pallas kernels  67.9 us (97%)
  local copies, waits for them, and re-layouts  1.32 us (2%)
    pallas_call x1, Pallas kernels, on_device(): pl.pallas_call(functools.partial(kernel, n_seq, n_shard, feats * n_shard,...  67.9 us

profile of v2, /device:TPU:0, one launch (start us, length us, event | category | flops | bytes accessed | tf_op | source)
XLA Modules:
  0.0 69.9 jit_solution(4819782327655770083)
XLA Ops:
  0.7 67.9 %shard_map.118 = f32[32,128]{1,0:T(8,128)} custom-call(bf16[128,1280]{1,0:T(8,128)(2,1)} %bitcast.12, bf16[128,1280]{1,0:T(8,128)(2,1)} %bitcast.13, bf16[128,1280]{1,0:T(8,128)(2,1)} %bitcast.14, bf16[128,2560]{1,0:T(8,128)(2,1)} %bitcast.11, bf16[1280,2560]{1,0:T(8,128)(2,1)} %w_hbm.1, f32[1,2560]{1,0:T(1,128)} %gate_hbm.1, f32[1,2560]{1,0:T(1,128)} %shift_hbm.1, ...), custom_call_target="tpu_custom_call" | custom-call | tf_op jit(solution)/shard_map/pallas_call | solution.py:334
  68.6 1.3 %copy.15 = f32[1,1,128,32]{2,3,1,0:T(8,128)} copy(f32[1,1,128,32]{2,3,1,0:T(8,128)} %bitcast.16) | data formatting | bytes 32768

commit v3 on v2

--- a/solution.py
+++ b/solution.py
@@ -111,9 +111,31 @@
         copy.start()
     pl.semaphore_wait(barrier, n_seq - 1 + n_local - 1)
 
+    def relay(t, side, step):
+        rows_from = block_rows(z - step if side == 0 else z + step)
+        source = left.at[t, rows_from]
+        if step == 0:
+            source = tensors[t + 1].at[:, pl.ds(left_at, n_left * HEAD_DIM)]
+        return pltpu.make_async_remote_copy(
+            src_ref=source, dst_ref=left.at[t, rows_from],
+            send_sem=l_send.at[t, side, step], recv_sem=l_recv.at[t, side, step],
+            device_id={"seq": z + 1 if side == 0 else z - 1}, device_id_type=MESH)
+
+    def relay_each(act, step):
+        for side in range(2):
+            at_source = z if side == 0 else n_seq - 1 - z
+            sends = jnp.logical_and(at_source >= step, at_source < n_seq - 1)
+            receives = at_source >= step + 1
+
+            @pl.when(receives if act == "wait_recv" else sends)
+            def _():
+                for t in range(2):
+                    getattr(relay(t, side, step), act)()
+
     order = sorted(range(1, n_seq), key=lambda d: -min(d, n_seq - d))
     z_copies = {}
-    for a in range(n_full):
+
+    def send_head(a):
         for d in order:
             for t in range(3):
                 copy = pltpu.make_async_remote_copy(
@@ -123,17 +145,11 @@
                     device_id={"seq": ahead(d)}, device_id_type=MESH)
                 copy.start()
                 z_copies[a, d, t] = copy
-    l_copies = []
+
     if n_left:
-        for d in order:
-            for t in range(2):
-                copy = pltpu.make_async_remote_copy(
-                    src_ref=tensors[t + 1].at[:, pl.ds(left_at, n_left * HEAD_DIM)],
-                    dst_ref=left.at[t, block_rows(z)],
-                    send_sem=l_send.at[t, d - 1], recv_sem=l_recv.at[t, d - 1],
-                    device_id={"seq": ahead(d)}, device_id_type=MESH)
-                copy.start()
-                l_copies.append(copy)
+        relay_each("start", 0)
+    if n_full:
+        send_head(0)
     for copy in loads:
         copy.start()
 
@@ -143,10 +159,27 @@
     consts = lax.dot_general(
         gains, wh_vm[...].astype(jnp.float32), (((1,), (1,)), ((), ())),
         precision=lax.Precision.HIGHEST, preferred_element_type=jnp.float32)
-    msg[me_local, rows:, :] = jnp.zeros((8, msg.shape[2]), jnp.float32)
-    msg[me_local, rows : rows + 2, 0:channels] = consts
+    msg[me_local, channels + 8 :, :] = jnp.zeros((8, rows), jnp.float32)
+    msg[me_local, channels + 8 : channels + 10, 0:channels] = consts
     for copy in own:
         copy.wait()
+
+    if n_left:
+        for step in range(n_seq - 2):
+            relay_each("wait_recv", step)
+            relay_each("start", step + 1)
+    for a in range(1, n_full):
+        for d in order:
+            for t in range(3):
+                z_copies[a - 1, d, t].wait_send()
+        send_head(a)
+
+    def attend_left():
+        relay_each("wait_recv", n_seq - 2)
+        for h in range(n_left):
+            cols = pl.ds(h * HEAD_DIM, HEAD_DIM)
+            att[g, :, pl.ds(left_at + h * HEAD_DIM, HEAD_DIM)] = attend(
+                q_left[:, cols], left[0, :, cols], left[1, :, cols])
 
     o_copies = []
     for a in range(n_full):
@@ -167,12 +200,10 @@
                     device_id={"seq": to}, device_id_type=MESH)
                 copy.start()
                 o_copies.append(copy)
-    for copy in l_copies:
-        copy.wait_recv()
-    for h in range(n_left):
-        cols = pl.ds(h * HEAD_DIM, HEAD_DIM)
-        att[g, :, pl.ds(left_at + h * HEAD_DIM, HEAD_DIM)] = attend(
-            q_left[:, cols], left[0, :, cols], left[1, :, cols])
+        if a == 0 and n_left:
+            attend_left()
+    if not n_full:
+        attend_left()
     for a in range(n_full):
         for d in range(1, n_seq):
             pltpu.make_async_remote_copy(
@@ -185,7 +216,6 @@
         device_id={"guide": 1 - g}, device_id_type=MESH)
     swap.start()
     loads[8].wait()
-    swap.wait_recv()
 
     def p_copy(b, q, c):
         return pltpu.make_async_remote_copy(
@@ -196,14 +226,14 @@
     def is_me(b, q):
         return jnp.logical_and(g == b, g * per + q == s)
 
-    both = jnp.concatenate([att[0], att[1]], axis=0)
-    for c in range(n_chunk):
-        for q in range(per):
-            part = jnp.dot(
-                both, w_vm[:, q * feats + c * chunk : q * feats + (c + 1) * chunk],
-                preferred_element_type=jnp.float32).astype(jnp.bfloat16)
-            for b in range(2):
-                psend[b, q, c] = part[b * rows : (b + 1) * rows]
+    for b in (g, 1 - g):
+        if b is not g:
+            swap.wait_recv()
+        for c in range(n_chunk):
+            for q in range(per):
+                psend[b, q, c] = jnp.dot(
+                    att[b], w_vm[:, q * feats + c * chunk : q * feats + (c + 1) * chunk],
+                    preferred_element_type=jnp.float32).astype(jnp.bfloat16)
 
                 @pl.when(is_me(b, q))
                 def _():
@@ -216,7 +246,7 @@
     from_guide = s // per
     first = jnp.zeros((rows, 1), jnp.float32)
     second = jnp.zeros((rows, 1), jnp.float32)
-    head = jnp.zeros((rows, channels), jnp.float32)
+    head = jnp.zeros((channels, rows), jnp.float32)
     for c in range(n_chunk):
         for r in range(n_shard):
 
@@ -242,11 +272,10 @@
         wh = wh_vm[:, at]
         for piece in (last, low, high):
             head = head + lax.dot_general(
-                piece, wh, (((1,), (1,)), ((), ())), preferred_element_type=jnp.float32)
-    msg[me_local, 0:rows, 0:channels] = head
-    tail = msg.shape[2] - channels
-    lane = lax.broadcasted_iota(jnp.int32, (rows, tail), 1)
-    msg[me_local, 0:rows, channels:] = jnp.where(lane == 0, first, second)
+                wh, piece, (((1,), (1,)), ((), ())), preferred_element_type=jnp.float32)
+    msg[me_local, 0:channels, :] = head
+    lane = lax.broadcasted_iota(jnp.int32, (rows, rows), 1)
+    msg[me_local, channels : channels + 8, :] = jnp.where(lane == 0, first, second).T[0:8]
     m_copies = []
     for d in range(1, n_local):
         copy = pltpu.make_async_remote_copy(
@@ -263,13 +292,12 @@
         total = msg[b]
         for r in range(1, n_shard):
             total = total + msg[r * 2 + b]
-        mean = total[0:rows, channels : channels + 1] / width_all
-        var = total[0:rows, channels + 1 : channels + 2] / width_all - mean * mean
+        mean = total[channels : channels + 1] / width_all
+        var = total[channels + 1 : channels + 2] / width_all - mean * mean
         inv = lax.rsqrt(var + norm_epsilon)
-        eps.append(
-            (total[0:rows, 0:channels] - mean * total[rows : rows + 1, 0:channels]) * inv
-            + total[rows + 1 : rows + 2, 0:channels])
-    guided = eps[1] + guidance_scale * (eps[0] - eps[1])
+        fixed = total[channels + 8 :].T[0:channels]
+        eps.append((total[0:channels] - fixed[:, 0:1] * mean) * inv + fixed[:, 1:2])
+    guided = (eps[1] + guidance_scale * (eps[0] - eps[1])).T
 
     f_copies = []
     for d in order + [0]:
@@ -297,7 +325,11 @@
     mine = jnp.where(is_first, frame[0:out_ch], frame[out_ch:])
     out_ref[...] = weight * (mine - noise_vm[...])
 
-    for copy in list(z_copies.values()) + l_copies + o_copies + m_copies + f_copies + [swap]:
+    last = [copy for (a, _, _), copy in z_copies.items() if a == n_full - 1]
+    if n_left:
+        for step in range(n_seq - 1):
+            relay_each("wait_send", step)
+    for copy in last + o_copies + m_copies + f_copies + [swap]:
         copy.wait_send()
     for c in range(n_chunk):
         for q in range(per):
@@ -351,11 +383,11 @@
             pltpu.VMEM((1, n_frame), jnp.int32),
             pltpu.VMEM((2, per, n_chunk, rows, chunk), bf16),
             pltpu.VMEM((n_shard, n_chunk, rows, chunk), bf16),
-            pltpu.VMEM((n_local, rows + 8, 128), f32),
+            pltpu.VMEM((n_local, channels + 16, rows), f32),
             pltpu.VMEM((n_seq, frame_rows, channels), f32),
             pltpu.VMEM((n_seq - 1, frame_rows, channels), f32),
             dma((full1, 3, n_seq - 1)), dma((full1, 3, n_seq - 1)),
-            dma((2, n_seq - 1)), dma((2, n_seq - 1)),
+            dma((2, 2, n_seq - 1)), dma((2, 2, n_seq - 1)),
             dma((full1, n_seq - 1)), dma((full1, n_seq - 1)),
             dma, dma,
             dma((2, per, n_chunk)), dma((n_shard, n_chunk)),

time: 70.2 us -> 67.2 us (0.957)
  Pallas kernels: 67.9 us -> 64.9 us
    pallas_call x1, Pallas kernels: 67.9 us -> 64.9 us  [on_device(): pl.pallas_call(functools.partial(kernel, n_seq, n_shard, feats * n_shard,...]
where the time goes in v3:
time: 67.2 us; the launch traced here: 66.9 us
  Pallas kernels  64.9 us (97%)
  local copies, waits for them, and re-layouts  1.32 us (2%)
    pallas_call x1, Pallas kernels, on_device(): pl.pallas_call(functools.partial(kernel, n_seq, n_shard, feats * n_shard,...  64.9 us

profile of v3, /device:TPU:0, one launch (start us, length us, event | category | flops | bytes accessed | tf_op | source)
XLA Modules:
  0.0 66.9 jit_solution(11408420500703699057)
XLA Ops:
  0.7 64.9 %shard_map.118 = f32[32,128]{1,0:T(8,128)} custom-call(bf16[128,1280]{1,0:T(8,128)(2,1)} %bitcast.12, bf16[128,1280]{1,0:T(8,128)(2,1)} %bitcast.13, bf16[128,1280]{1,0:T(8,128)(2,1)} %bitcast.14, bf16[128,2560]{1,0:T(8,128)(2,1)} %bitcast.11, bf16[1280,2560]{1,0:T(8,128)(2,1)} %w_hbm.1, f32[1,2560]{1,0:T(1,128)} %gate_hbm.1, f32[1,2560]{1,0:T(1,128)} %shift_hbm.1, ...), custom_call_target="tpu_custom_call" | custom-call | tf_op jit(solution)/shard_map/pallas_call | solution.py:366
  65.6 1.3 %copy.15 = f32[1,1,128,32]{2,3,1,0:T(8,128)} copy(f32[1,1,128,32]{2,3,1,0:T(8,128)} %bitcast.16) | data formatting | bytes 32768
